TPU v7x, 32 devices: a whole 2x2x4 slice. The times are simulated.
32 devices in a mesh: dp: 16 (over z, x, core), mp: 2 (over y).
Axes of the slice: x: 2, y: 2, z: 4, core: 2. Of those that a mesh axis runs over, the one named last changes fastest.
Arguments:
- tokens: bfloat16 [6400, 1792], P('dp', 'mp'), may hold values from -6 to 6
- cotangent: bfloat16 [6400, 1792], P('dp', 'mp'), may hold values from -6 to 6
- master: float32 [1792, 4, 1792], P('dp', None, 'mp')
- moment_one: float32 [1792, 4, 1792], P('dp', None, 'mp'), may hold values from -4 to 4
- moment_two: float32 [1792, 4, 1792], P('dp', None, 'mp'), may hold values from 0.01 to 1
- ln_gain: float32 [1792], replicated, may hold values from 0.1 to 1.9
- ln_bias: float32 [1792], replicated, may hold values from -3 to 3
- norm_moment_one: float32 [2, 1792], replicated, may hold values from -4 to 4
- norm_moment_two: float32 [2, 1792], replicated, may hold values from 0.01 to 1
- image_count: int32 [16], P('dp'), may hold values from 1 to 25, as said below
- tokens_per_image: int32 [16], P('dp'), may hold values from 16 to 400, as said below
Outputs:
- block_out: bfloat16 [6400, 1792], P('dp', 'mp')
- input_grad: bfloat16 [6400, 1792], P('dp', 'mp')
- new_master: float32 [1792, 4, 1792], P('dp', None, 'mp')
- new_moment_one: float32 [1792, 4, 1792], P('dp', None, 'mp')
- new_moment_two: float32 [1792, 4, 1792], P('dp', None, 'mp')
- new_gain: float32 [1792], replicated
- new_bias: float32 [1792], replicated
- new_norm_moment_one: float32 [2, 1792], replicated
- new_norm_moment_two: float32 [2, 1792], replicated
Inputs may be any that keep to these rules, and one draw needn't show every extreme that they name: `tokens_per_image`: A square number s * s; some group has exactly 400. image_count[g] * tokens_per_image[g] is at most 400 for every group g.
All inputs are finite; a program needn't handle non-finite values.
Results may differ from a plain program's by a relative error of at most 0.0085.
Values may be sent and summed in bfloat16 or wider, within the bound.
No kernel may reach another device: no remote copies, remote signals or barrier semaphores. Data moves between devices by JAX's collectives and lax.ppermute only.
A program may use at most 192 MiB of HBM per device.

v0:
```python
import jax
import jax.numpy as jnp
from jax import lax
from jax.sharding import PartitionSpec as P

HEAD_DIM = 112


eps_norm = 1e-06
beta_one = 0.9
beta_two = 0.95
learn_rate = 0.01
decay_rate = 0.1
adam_eps = 1e-08
step_count = 10.0


def layer_norm(row_block, gain, shift):
    values = row_block.astype(jnp.float32)
    center = jnp.mean(values, axis=-1, keepdims=True)
    shifted = values - center
    spread = jnp.mean(shifted * shifted, axis=-1, keepdims=True)
    inverse = lax.rsqrt(spread + eps_norm)
    normed = shifted * inverse
    return (normed, inverse, (normed * gain + shift).astype(jnp.bfloat16))


def same_image(image_here, length_here, total_rows):
    places = jnp.arange(total_rows, dtype=jnp.int32)
    live_rows = places < image_here * length_here
    labels = jnp.where(live_rows, places // length_here, jnp.int32(-1))
    return (live_rows, labels[:, None] == labels[None, :])


def adam_update(weight_now, moment_first, moment_second, gradient, decay):
    first_new = beta_one * moment_first + (1.0 - beta_one) * gradient
    second_new = beta_two * moment_second + (1.0 - beta_two) * gradient * gradient
    first_hat = first_new / (1.0 - beta_one**step_count)
    second_hat = second_new / (1.0 - beta_two**step_count)
    weight_new = weight_now - learn_rate * (
        first_hat / (jnp.sqrt(second_hat) + adam_eps) + decay * weight_now
    )
    return (weight_new, first_new, second_new)


def shards(
    tokens,
    cotangent,
    master,
    moment_one,
    moment_two,
    ln_gain,
    ln_bias,
    norm_moment_one,
    norm_moment_two,
    image_count,
    tokens_per_image,
):
    groups = lax.axis_size("dp")
    full_tokens, full_cot = (
        lax.all_gather(tokens, "mp", axis=1, tiled=True),
        lax.all_gather(cotangent, "mp", axis=1, tiled=True),
    )
    row_count = full_tokens.shape[0]
    normed, inverse, normed_low = layer_norm(full_tokens, ln_gain, ln_bias)
    live_rows, allowed = same_image(image_count[0], tokens_per_image[0], row_count)
    weights = lax.all_gather(master.astype(jnp.bfloat16), "dp", axis=0, tiled=True)
    heads_here = weights.shape[2] // HEAD_DIM
    score_scale = HEAD_DIM ** (-0.5)
    projected = jnp.einsum(
        "td,dkh->kth", normed_low, weights[:, :3], preferred_element_type=jnp.float32
    ).astype(jnp.bfloat16)
    query_rows = projected[0].reshape(row_count, heads_here, HEAD_DIM)
    key_rows = projected[1].reshape(row_count, heads_here, HEAD_DIM)
    value_rows = projected[2].reshape(row_count, heads_here, HEAD_DIM)
    scores = (
        jnp.einsum("qhd,khd->hqk", query_rows, key_rows, preferred_element_type=jnp.float32)
        * score_scale
    )
    scores = jnp.where(allowed[None], scores, -1e30)
    row_max = jnp.max(scores, axis=-1, keepdims=True)
    raised = jnp.exp(scores - row_max)
    prob_full = raised / jnp.sum(raised, axis=-1, keepdims=True)
    prob_half = prob_full.astype(jnp.bfloat16)
    mixed = jnp.einsum(
        "hqk,khd->qhd", prob_half, value_rows, preferred_element_type=jnp.float32
    ).astype(jnp.bfloat16)
    mixed = mixed.reshape(row_count, heads_here * HEAD_DIM)
    out_weight = weights[:, 3]
    out_part = lax.dot_general(
        mixed, out_weight, (((1,), (1,)), ((), ())), preferred_element_type=jnp.float32
    )
    out_sum = lax.psum_scatter(
        out_part.astype(jnp.bfloat16), "mp", scatter_dimension=1, tiled=True
    ).astype(jnp.float32)
    block_out = (tokens.astype(jnp.float32) + out_sum).astype(jnp.bfloat16)
    live_column = live_rows[:, None]
    grad_full = jnp.where(live_column, full_cot, jnp.zeros_like(full_cot))
    mixed_grad = jnp.dot(grad_full, out_weight, preferred_element_type=jnp.float32).astype(
        jnp.bfloat16
    )
    mixed_grad = mixed_grad.reshape(row_count, heads_here, HEAD_DIM)
    prob_grad = jnp.einsum(
        "qhd,khd->hqk", mixed_grad, value_rows, preferred_element_type=jnp.float32
    )
    value_grad = jnp.einsum(
        "hqk,qhd->khd", prob_half, mixed_grad, preferred_element_type=jnp.float32
    ).astype(jnp.bfloat16)
    delta = jnp.sum(prob_full * prob_grad, axis=-1, keepdims=True)
    score_grad = (prob_full * (prob_grad - delta) * score_scale).astype(jnp.bfloat16)
    query_grad = jnp.einsum(
        "hqk,khd->qhd", score_grad, key_rows, preferred_element_type=jnp.float32
    ).astype(jnp.bfloat16)
    key_grad = jnp.einsum(
        "hqk,qhd->khd", score_grad, query_rows, preferred_element_type=jnp.float32
    ).astype(jnp.bfloat16)
    proj_grad = jnp.stack([query_grad, key_grad, value_grad]).reshape(
        3, row_count, heads_here * HEAD_DIM
    )
    norm_grad = jnp.einsum(
        "kth,dkh->td", proj_grad, weights[:, :3], preferred_element_type=jnp.float32
    )
    gain_part = jnp.sum(norm_grad * normed, axis=0)
    bias_part = jnp.sum(norm_grad, axis=0)
    scaled = norm_grad * ln_gain
    input_part = inverse * (
        scaled
        - jnp.mean(scaled, axis=-1, keepdims=True)
        - normed * jnp.mean(scaled * normed, axis=-1, keepdims=True)
    )
    input_sum = lax.psum_scatter(
        input_part.astype(jnp.bfloat16), "mp", scatter_dimension=1, tiled=True
    ).astype(jnp.float32)
    grad_local = jnp.where(live_column, cotangent, jnp.zeros_like(cotangent))
    input_grad = (grad_local.astype(jnp.float32) + input_sum).astype(jnp.bfloat16)
    gain_sum, bias_sum = lax.psum((gain_part, bias_part), ("dp", "mp"))
    inner_grad = jnp.einsum(
        "td,kth->dkh", normed_low, proj_grad, preferred_element_type=jnp.float32
    )
    out_grad = lax.dot_general(
        grad_full, mixed, (((0,), (0,)), ((), ())), preferred_element_type=jnp.float32
    )
    full_grad = jnp.concatenate([inner_grad, out_grad[:, None]], axis=1)
    grad_shard = lax.psum_scatter(full_grad, "dp", scatter_dimension=0, tiled=True)
    weight_grad = grad_shard / groups
    new_master, new_moment_one, new_moment_two = adam_update(
        master, moment_one, moment_two, weight_grad, decay_rate
    )
    norm_param_grad = jnp.stack([gain_sum, bias_sum]) / groups
    stacked_params = jnp.stack([ln_gain, ln_bias])
    new_norm, new_norm_moment_one, new_norm_moment_two = adam_update(
        stacked_params, norm_moment_one, norm_moment_two, norm_param_grad, 0.0
    )
    return (
        block_out,
        input_grad,
        new_master,
        new_moment_one,
        new_moment_two,
        new_norm[0],
        new_norm[1],
        new_norm_moment_one,
        new_norm_moment_two,
    )


def solution(mesh):
    return jax.shard_map(
        shards,
        mesh=mesh,
        in_specs=(
            P("dp", "mp"),
            P("dp", "mp"),
            P("dp", None, "mp"),
            P("dp", None, "mp"),
            P("dp", None, "mp"),
            P(),
            P(),
            P(),
            P(),
            P("dp"),
            P("dp"),
        ),
        out_specs=(
            P("dp", "mp"),
            P("dp", "mp"),
            P("dp", None, "mp"),
            P("dp", None, "mp"),
            P("dp", None, "mp"),
            P(),
            P(),
            P(),
            P(),
        ),
        check_vma=False,
    )
```

profile of v0, /device:TPU:0, one launch (start us, length us, event | category | flops | bytes accessed | tf_op | source)
XLA Modules:
  0.0 542.3 jit_solution(10332074574319555309)
XLA Ops:
  7.2 0.7 all-gather.4.cloned.1.call-update
  8.0 2.4 copy.112
  10.4 0.7 all-gather.8.cloned.1.call-update
  12.8 25.1 %all-gather.4.cloned.1.call-done = bf16[400,1792]{1,0:T(8,128)(2,1)} async-done(((bf16[400,896]{1,0:T(8,128)(2,1)}), bf16[400,1792]{1,0:T(8,128)(2,1)}) %all-gather.4.cloned.1.call-update) | async-done | bytes 1433616 | tf_op jit(solution)/shard_map/all_gather | solution.py:61
  37.9 1.7 convert_reduce_fusion
  39.7 1.9 fusion.35
  41.6 101.6 %all-gather.6.cloned.1.call-done = bf16[1792,4,896]{2,0,1:T(8,128)(2,1)} async-done(((bf16[112,4,896]{2,0,1:T(8,128)(2,1)}), bf16[1792,4,896]{2,0,1:T(8,128)(2,1)}) %all-gather.6.cloned.1.call-update) | async-done | bytes 12845072 | tf_op jit(solution)/shard_map/all_gather | solution.py:67
  143.1 8.2 %convert_bitcast_fusion = bf16[3,400,896]{2,1,0:T(8,128)(2,1)S(1)} fusion(bf16[1792,4,896]{2,0,1:T(8,128)(2,1)} %all-gather.6.cloned.1.call-done, bf16[400,1792]{1,0:T(8,128)(2,1)S(1)} %copy-done, f32[1792]{0:T(1024)S(1)} %copy-done.14, f32[1792]{0:T(1024)S(1)} %copy-done.11, f32[400]{0:T(512)S(1)} %add_rsqrt_fusion, f32[400]{0:T(512)S(1)} %broadcast_multiply_fusion.2), kind=kOutput, calls=%fused_computation.42 | convolution fusion | flops 3858892800 | bytes 13235328 | tf_op jit(solution)/shard_map/td,dkh->kth/dot_general | solution.py:70
  151.4 1.0 fusion.98
  152.4 1.8 reshape_squeeze.9
  154.2 0.9 reshape_squeeze.11
  155.1 2.6 reshape_squeeze.10
  157.8 10.7 %all-gather.8.cloned.1.call-done = bf16[400,1792]{1,0:T(8,128)(2,1)} async-done(((bf16[400,896]{1,0:T(8,128)(2,1)}), bf16[400,1792]{1,0:T(8,128)(2,1)}) %all-gather.8.cloned.1.call-update) | async-done | bytes 1433616 | tf_op jit(solution)/shard_map/all_gather | solution.py:62
  168.5 4.9 fusion.60
  173.4 2.8 reshape.118
  176.2 1.0 fusion.79
  177.3 2.6 fusion.99
  179.9 4.1 fusion.74
  184.1 1.3 fusion.64
  185.4 1.9 fusion.61
  187.5 1.5 reshape.117
  189.1 4.9 fusion.38
  194.0 3.7 copy.84
  198.0 13.2 %fusion.70 = bf16[400,8,112]{2,0,1:T(8,128)(2,1)} fusion(f32[8,400,400]{1,2,0:T(8,128)} %fusion.74, bf16[400,8,112]{2,1,0:T(8,128)(2,1)S(1)} %copy-done.3, f32[8,400,400]{1,2,0:T(8,128)} %copy-done.15, f32[8,400]{1,0:T(8,128)S(1)} %get-tuple-element.53), kind=kOutput, calls=%fused_computation.65 | convolution fusion | flops 296041984 | bytes 11686400 | tf_op jit(solution)/shard_map/hqk,khd->qhd/dot_general | solution.py:111
  211.2 1.4 copy.70
  212.5 1.5 stack.26
  214.1 10.9 %fusion.67 = bf16[400,8,112]{2,0,1:T(8,128)(2,1)} fusion(f32[8,400,400]{1,2,0:T(8,128)} %fusion.74, bf16[400,8,112]{2,1,0:T(8,128)(2,1)S(1)} %reshape_squeeze.10, f32[8,400,400]{1,2,0:T(8,128)} %copy-done.15, f32[8,400]{1,0:T(8,128)S(1)} %get-tuple-element.53), kind=kOutput, calls=%fused_computation.64 | convolution fusion | flops 296041984 | bytes 11686400 | tf_op jit(solution)/shard_map/hqk,qhd->khd/dot_general | solution.py:114
  224.9 1.4 copy.72
  226.4 1.5 stack.27
  227.9 1.4 copy.74
  229.3 1.5 stack.28
  230.9 1.3 constant_dynamic-update-slice_fusion.1
  232.2 8.8 %fusion.34 = (f32[1792]{0:T(1024)S(1)}, f32[400]{0:T(512)S(1)}, f32[400]{0:T(512)S(1)}, f32[1792]{0:T(1024)S(1)}, f32[400,1792]{1,0:T(8,128)S(1)}) fusion(bf16[400,1792]{1,0:T(8,128)(2,1)S(1)} %copy-done, f32[400]{0:T(512)S(1)} %add_rsqrt_fusion, f32[400]{0:T(512)S(1)} %broadcast_multiply_fusion.2, f32[1792]{0:T(1024)S(1)} %copy-done.11, ...), kind=kOutput, calls=%fused_computation.36 | convolution fusion | flops 3860680192 | bytes 16112896 | tf_op jit(solution)/shard_map/kth,dkh->td/dot_general | solution.py:120
  241.1 0.9 fusion.33
  242.0 2.3 copy.86
  244.7 3.9 convolution_bitcast_fusion
  248.6 5.7 %fusion.83 = f32[1792,3,896]{2,0,1:T(8,128)S(1)} fusion(bf16[3,400,896]{2,1,0:T(8,128)(2,1)S(1)} %copy-done.10, bf16[400,1792]{1,0:T(8,128)(2,1)S(1)} %copy-done, f32[1792]{0:T(1024)S(1)} %copy-done.14, f32[1792]{0:T(1024)S(1)} %copy-done.11, f32[400]{0:T(512)S(1)} %add_rsqrt_fusion, f32[400]{0:T(512)S(1)} %broadcast_multiply_fusion.2), kind=kOutput, calls=%fused_computation.77 | convolution fusion | flops 3857817600 | bytes 22869120 | tf_op jit(solution)/shard_map/td,kth->dkh/dot_general | solution.py:137
  254.3 8.8 %pad_maximum_fusion = f32[1792,4,896]{2,0,1:T(8,128)} fusion(f32[1792,1,896]{2,0,1:T(8,128)S(1)} %convolution_bitcast_fusion, f32[1792,3,896]{2,0,1:T(8,128)S(1)} %fusion.83), kind=kLoop, calls=%fused_computation.2 | loop fusion | flops 6422528 | bytes 51380224 | tf_op jit(solution)/shard_map/concatenate | solution.py:143
  263.1 39.9 %all-reduce = (f32[1,1792]{1,0:T(1,128)S(1)}, f32[1,1792]{1,0:T(1,128)S(1)}) all-reduce(f32[1,1792]{1,0:T(1,128)S(1)} %stack.32, f32[1,1792]{1,0:T(1,128)S(1)} %stack.31), channel_id=1, replica_groups=mesh['dp'=16,'mp'=2] {'dp','mp'}, use_global_device_ids=true, to_apply=%region_13.14 | all-reduce | flops 3584 | bytes 28672 | tf_op jit(solution)/shard_map/psum | solution.py:136
  304.4 2.3 copy.85
  306.7 2.0 copy.87
  308.6 2.7 add_convert_fusion.1
  311.4 1.1 add_convert_fusion
  312.5 213.8 %reduce-scatter.8.cloned.1.call-done = f32[112,4,896]{2,0,1:T(8,128)} async-done(((f32[1792,4,896]{2,0,1:T(8,128)}), f32[112,4,896]{2,0,1:T(8,128)}) %reduce-scatter.8.cloned.1.call-update) | async-done | bytes 1605648 | tf_op jit(solution)/shard_map/reduce_scatter | solution.py:144
  526.3 3.7 multiply_subtract_fusion
  529.9 1.8 copy.79
  531.7 1.8 copy.80
  533.5 1.8 copy.81
  (59 shorter events, 2.8 us)
Async XLA Ops:
  7.2 30.8 %all-gather.4.cloned.1.call-start = ((), (), s32[]{:S(2)}) async-start(), calls=%async_computation.3 | async-start | bytes 2150400 | tf_op jit(solution)/shard_map/all_gather | solution.py:61
  7.9 135.2 %all-gather.6.cloned.1.call-start = ((), (), s32[]{:S(2)}) async-start(), calls=%async_computation.4 | async-start | bytes 13647872 | tf_op jit(solution)/shard_map/all_gather | solution.py:67
  10.4 132.8 %copy-start.11 = (f32[1792]{0:T(1024)S(1)}, f32[1792]{0:T(1024)}, u32[]{:S(2)}) copy-start(f32[1792]{0:T(1024)} %param.16) | copy-start | bytes 21508
  10.4 132.8 %copy-start.14 = (f32[1792]{0:T(1024)S(1)}, f32[1792]{0:T(1024)}, u32[]{:S(2)}) copy-start(f32[1792]{0:T(1024)} %param.17) | copy-start | bytes 21508
  10.4 158.1 %all-gather.8.cloned.1.call-start = ((), (), s32[]{:S(2)}) async-start(), calls=%async_computation.5 | async-start | bytes 2150400 | tf_op jit(solution)/shard_map/all_gather | solution.py:62
  11.1 293.2 %reduce-scatter.10.cloned.1.call-start = ((), (), s32[]{:S(2)}) async-start(), calls=%async_computation.7 | async-start | bytes 2752512
  37.9 105.2 %copy-start = (bf16[400,1792]{1,0:T(8,128)(2,1)S(1)}, bf16[400,1792]{1,0:T(8,128)(2,1)}, u32[]{:S(2)}) copy-start(bf16[400,1792]{1,0:T(8,128)(2,1)} %all-gather.4.cloned.1.call-done) | copy-start | bytes 4300804
  155.1 21.1 %copy-start.2 = (bf16[400,8,112]{2,1,0:T(8,128)(2,1)}, bf16[400,8,112]{2,1,0:T(8,128)(2,1)S(1)}, u32[]{:S(2)}) copy-start(bf16[400,8,112]{2,1,0:T(8,128)(2,1)S(1)} %reshape_squeeze.11) | copy-start | bytes 2150404
  177.2 2.6 copy-start.4
  177.3 2.6 copy-start.5
  179.9 5.5 %copy-start.15 = (f32[8,400,400]{1,2,0:T(8,128)}, f32[8,400,400]{1,2,0:T(8,128)S(1)}, u32[]{:S(2)}) copy-start(f32[8,400,400]{1,2,0:T(8,128)S(1)} %get-tuple-element.54) | copy-start | bytes 15360004
  194.0 4.0 copy-start.3
  197.7 108.9 %reduce-scatter.12.cloned.1.call-start = ((), (), s32[]{:S(2)}) async-start(), calls=%async_computation.8 | async-start | bytes 2752512
  224.9 5.9 %copy-start.7 = (bf16[1,400,896]{2,1,0:T(8,128)(2,1)S(1)}, bf16[1,400,896]{2,1,0:T(8,128)(2,1)}, u32[]{:S(2)}) copy-start(bf16[1,400,896]{2,1,0:T(8,128)(2,1)} %stack.26) | copy-start | bytes 2150404
  230.8 1.3 copy-start.8
  232.2 8.8 %copy-start.9 = (bf16[3,400,896]{2,1,0:T(8,128)(2,1)}, bf16[3,400,896]{2,1,0:T(8,128)(2,1)S(1)}, u32[]{:S(2)}) copy-start(bf16[3,400,896]{2,1,0:T(8,128)(2,1)S(1)} %constant_dynamic-update-slice_fusion) | copy-start | bytes 6451204
  244.4 281.9 %reduce-scatter.8.cloned.1.call-start = ((), (), s32[]{:S(2)}) async-start(), calls=%async_computation.6 | async-start | bytes 27295744 | tf_op jit(solution)/shard_map/reduce_scatter | solution.py:144
  244.7 3.9 copy-start.10
  263.0 40.0 %copy-start.12 = (f32[2,1792]{1,0:T(2,128)S(1)}, f32[2,1792]{1,0:T(2,128)}, u32[]{:S(2)}) copy-start(f32[2,1792]{1,0:T(2,128)} %param.18) | copy-start | bytes 43012
  263.0 40.0 %copy-start.13 = (f32[2,1792]{1,0:T(2,128)S(1)}, f32[2,1792]{1,0:T(2,128)}, u32[]{:S(2)}) copy-start(f32[2,1792]{1,0:T(2,128)} %param.19) | copy-start | bytes 43012
  263.1 48.3 %copy-start.6 = (bf16[400,896]{1,0:T(8,128)(2,1)S(1)}, bf16[400,896]{1,0:T(8,128)(2,1)}, u32[]{:S(2)}) copy-start(bf16[400,896]{1,0:T(8,128)(2,1)} %param.12) | copy-start | bytes 2150404
  306.7 219.6 %copy-start.1 = (f32[112,4,896]{2,1,0:T(4,128)S(1)}, f32[112,4,896]{2,1,0:T(4,128)}, u32[]{:S(2)}) copy-start(f32[112,4,896]{2,1,0:T(4,128)} %param.13) | copy-start | bytes 4816900
Sparse Core Ops, SparseCore 0:
  9.6 28.3 all-gather.3
  40.7 102.3 all-gather.5
  144.7 23.7 all-gather.7
  197.9 28.9 reduce-scatter.9
  244.5 29.4 reduce-scatter.11
  278.0 248.1 reduce-scatter.7
where the time goes:
time: 548 us; the launch traced here: 542 us
  waiting for transfers between devices  353 us (64%)
  matrix products  68.8 us (13%)
  local copies, waits for them, and re-layouts  39.9 us (7%)
  blocking collectives  39.9 us (7%)
  other arithmetic  24.5 us (4%)
  between operations  16 us (3%)
    reduce_scatter x1, waiting for transfers between devices, shards(): lax.psum_scatter(full_grad, 'dp', scatter_dimension=0, tiled=True)  214 us
    all_gather x1, waiting for transfers between devices, shards(): lax.all_gather(master.astype(jnp.bfloat16), 'dp', axis=0, tiled=True)  102 us
    psum x1, blocking collectives, shards(): gain_sum, bias_sum = lax.psum((gain_part, bias_part), ('dp', 'mp'))  39.9 us
    all_gather x1, waiting for transfers between devices, shards(): lax.all_gather(tokens, 'mp', axis=1, tiled=True)  25.1 us
    unnamed x42, local copies, waits for them, and re-layouts  19.4 us
    dot_general x1, matrix products, shards(): jnp.einsum('hqk,khd->qhd', score_grad, key_rows, preferred_element_type=j...  13.2 us
  transfers between devices with their start and end apart: 6, of which 4 were waited for; matrix products, arithmetic and copies ran while one was open for 18% of the time, Pallas kernels for 0%

commit v1 on v0

v1 whole, which is shorter than its diff:
```python
import functools

import jax
import jax.numpy as jnp
from jax import lax
from jax.experimental import pallas as pl
from jax.experimental.pallas import tpu as pltpu
from jax.sharding import PartitionSpec as P

HEAD_DIM = 112
LANES = 128

eps_norm = 1e-06
beta_one = 0.9
beta_two = 0.95
learn_rate = 0.01
decay_rate = 0.1
adam_eps = 1e-08
step_count = 10.0

bf16 = jnp.bfloat16
f32 = jnp.float32
WHOLE = pl.BlockSpec(memory_space=pltpu.VMEM)
SCALARS = pl.BlockSpec(memory_space=pltpu.SMEM)
ANYWHERE = pl.BlockSpec(memory_space=pl.ANY)
BIG = pltpu.CompilerParams(vmem_limit_bytes=56 * 1024 * 1024)


def round_up(value, unit):
    return -(-value // unit) * unit


def nt_dot(left, right):
    return lax.dot_general(left, right, (((1,), (1,)), ((), ())), preferred_element_type=f32)


def nn_dot(left, right):
    return jnp.dot(left, right, preferred_element_type=f32)


def layer_norm(row_block, gain, shift):
    values = row_block.astype(f32)
    center = jnp.mean(values, axis=-1, keepdims=True)
    shifted = values - center
    spread = jnp.mean(shifted * shifted, axis=-1, keepdims=True)
    inverse = lax.rsqrt(spread + eps_norm)
    normed = shifted * inverse
    return (normed, inverse, (normed * gain + shift).astype(bf16))


def adam_update(weight_now, moment_first, moment_second, gradient, decay):
    first_new = beta_one * moment_first + (1.0 - beta_one) * gradient
    second_new = beta_two * moment_second + (1.0 - beta_two) * gradient * gradient
    first_hat = first_new / (1.0 - beta_one**step_count)
    second_hat = second_new / (1.0 - beta_two**step_count)
    weight_new = weight_now - learn_rate * (
        first_hat / (jnp.sqrt(second_hat) + adam_eps) + decay * weight_now
    )
    return (weight_new, first_new, second_new)


class Plan:
    def __init__(self, columns):
        self.kind = columns // 2
        self.both = 2 * self.kind
        self.start = self.kind // LANES * LANES
        self.base = self.kind - self.start
        self.wide = self.both - self.start
        self.heads = self.kind // HEAD_DIM

    def window(self, head, base):
        low = base + head * HEAD_DIM
        high = low + HEAD_DIM
        return (low // LANES * LANES, min(self.wide, round_up(high, LANES)), low, high)


def pack_kernel(plan, master_ref, *outs):
    for chunk in range(2):
        for pair, kinds in enumerate(((0, 3), (1, 2))):
            columns = [
                master_ref[:, kind, chunk * plan.kind : (chunk + 1) * plan.kind] for kind in kinds
            ]
            outs[2 * chunk + pair][...] = jnp.concatenate(columns, axis=1).astype(bf16)


def pack(plan, master):
    out = jax.ShapeDtypeStruct((master.shape[0], plan.both), bf16)
    return pl.pallas_call(
        functools.partial(pack_kernel, plan),
        out_shape=[out] * 4,
        in_specs=[WHOLE],
        out_specs=[WHOLE] * 4,
        compiler_params=BIG,
        name="pack",
    )(master)


def project_kernel(plan, count, place_ref, normed_ref, grad_ref, *rest):
    blocks, rest = rest[: 2 * count], rest[2 * count :]
    query_ref, key_ref, value_ref, mixed_grad_ref, full_qo, full_kv, held_qo, held_kv, sems, outs = rest
    held = (held_qo, held_kv)
    rows = blocks[0].shape[0]
    copies = []
    for pair in range(2):
        for at in range(count):
            first = place_ref[at] * rows
            if rows % 16 == 0:
                first = pl.multiple_of(first, 16)
            copy = pltpu.make_async_copy(
                blocks[pair * count + at], held[pair].at[pl.ds(first, rows)], sems.at[pair * count + at]
            )
            copy.start()
            copies.append(copy)
    left, right = slice(0, plan.wide), slice(plan.start, plan.both)
    live = lax.broadcasted_iota(jnp.int32, (1, plan.wide), 1) >= plan.base
    for copy in copies[:count]:
        copy.wait()
    keep_qo = pltpu.make_async_copy(held_qo, full_qo, outs.at[0])
    keep_qo.start()
    query_ref[...] = nn_dot(normed_ref[...], held_qo[:, left]).astype(bf16)
    mixed_grad = nn_dot(grad_ref[...], held_qo[:, right])
    mixed_grad_ref[...] = jnp.where(live, mixed_grad, 0.0).astype(bf16)
    for copy in copies[count:]:
        copy.wait()
    keep_kv = pltpu.make_async_copy(held_kv, full_kv, outs.at[1])
    keep_kv.start()
    key_ref[...] = nn_dot(normed_ref[...], held_kv[:, left]).astype(bf16)
    value_ref[...] = nn_dot(normed_ref[...], held_kv[:, right]).astype(bf16)
    keep_qo.wait()
    keep_kv.wait()


def project(plan, places, normed_low, grad_rows, blocks):
    count = len(blocks) // 2
    rows, depth = normed_low.shape
    out = jax.ShapeDtypeStruct((rows, plan.wide), bf16)
    full = jax.ShapeDtypeStruct((depth, plan.both), bf16)
    return pl.pallas_call(
        functools.partial(project_kernel, plan, count),
        out_shape=[out] * 4 + [full] * 2,
        in_specs=[SCALARS, WHOLE, WHOLE] + [ANYWHERE] * (2 * count),
        out_specs=[WHOLE] * 4 + [ANYWHERE] * 2,
        scratch_shapes=[
            pltpu.VMEM((depth, plan.both), bf16),
            pltpu.VMEM((depth, plan.both), bf16),
            pltpu.SemaphoreType.DMA((2 * count,)),
            pltpu.SemaphoreType.DMA((2,)),
        ],
        compiler_params=BIG,
        cost_estimate=pl.CostEstimate(
            flops=8 * rows * depth * plan.wide, bytes_accessed=8 * depth * plan.both, transcendentals=0
        ),
        name="project",
    )(places, normed_low, grad_rows, *blocks)


def attend_kernel(
    plan, key_label_ref, query_label_ref, query_ref, key_ref, value_ref, mixed_grad_ref,
    mixed_ref, query_grad_ref, key_grad_ref, value_grad_ref, mixed_turned, query_turned, key_sum, value_sum,
):
    rows = query_ref.shape[0]
    padded = query_label_ref.shape[1]
    scale = HEAD_DIM ** (-0.5)
    fill = jnp.zeros((padded - rows, plan.wide), bf16)
    query = jnp.concatenate([query_ref[...], fill], axis=0)
    mixed_grad = jnp.concatenate([mixed_grad_ref[...], fill], axis=0)
    key_turned = jnp.concatenate([key_ref[...], fill], axis=0).T
    value_turned = jnp.concatenate([value_ref[...], fill], axis=0).T
    allowed = key_label_ref[...] == query_label_ref[...]
    mixed_turned[...] = jnp.zeros_like(mixed_turned)
    query_turned[...] = jnp.zeros_like(query_turned)
    key_sum[...] = jnp.zeros_like(key_sum)
    value_sum[...] = jnp.zeros_like(value_sum)
    zero = jnp.zeros((), bf16)
    for head in range(plan.heads):
        a, b, low, high = plan.window(head, 0)
        c, d, low_v, high_v = plan.window(head, plan.base)
        lane = a + lax.broadcasted_iota(jnp.int32, (1, b - a), 1)
        lane_v = c + lax.broadcasted_iota(jnp.int32, (1, d - c), 1)
        here = (lane >= low) & (lane < high)
        here_v = (lane_v >= low_v) & (lane_v < high_v)
        queries = jnp.where(here, query[:, a:b], zero)
        grads = jnp.where(here_v, mixed_grad[:, c:d], zero)
        scores = jnp.where(allowed, nt_dot(key_ref[:, a:b], queries) * scale, -1e30)
        raised = jnp.exp(scores - jnp.max(scores, axis=0, keepdims=True))
        prob = raised * (1.0 / jnp.sum(raised, axis=0, keepdims=True))
        prob_half = prob.astype(bf16)
        prob_grad = nt_dot(value_ref[:, c:d], grads)
        delta = jnp.sum(prob * prob_grad, axis=0, keepdims=True)
        score_grad = (prob * (prob_grad - delta) * scale).astype(bf16)
        row = a + lax.broadcasted_iota(jnp.int32, (b - a, 1), 0)
        row_v = c + lax.broadcasted_iota(jnp.int32, (d - c, 1), 0)
        mixed_part = nn_dot(value_turned[c:d, :rows], prob_half)
        mixed_turned[c:d, :] += jnp.where((row_v >= low_v) & (row_v < high_v), mixed_part, 0.0)
        query_part = nn_dot(key_turned[a:b, :rows], score_grad)
        query_turned[a:b, :] += jnp.where((row >= low) & (row < high), query_part, 0.0)
        value_sum[:, c:d] += nn_dot(prob_half, grads)
        key_sum[:, a:b] += nn_dot(score_grad, queries)
    mixed_ref[...] = mixed_turned[...].T.astype(bf16)
    query_grad_ref[...] = query_turned[...].T.astype(bf16)
    key_grad_ref[...] = jnp.concatenate([key_sum[...].astype(bf16), fill], axis=0)
    value_grad_ref[...] = jnp.concatenate([value_sum[...].astype(bf16), fill], axis=0)


def attend(plan, key_labels, query_labels, query, key, value, mixed_grad):
    rows = query.shape[0]
    padded = query_labels.shape[1]
    out = jax.ShapeDtypeStruct((padded, plan.wide), bf16)
    return pl.pallas_call(
        functools.partial(attend_kernel, plan),
        out_shape=[out] * 4,
        in_specs=[WHOLE] * 6,
        out_specs=[WHOLE] * 4,
        scratch_shapes=[
            pltpu.VMEM((plan.wide, padded), f32),
            pltpu.VMEM((plan.wide, padded), f32),
            pltpu.VMEM((rows, plan.wide), f32),
            pltpu.VMEM((rows, plan.wide), f32),
        ],
        compiler_params=BIG,
        cost_estimate=pl.CostEstimate(
            flops=16 * plan.heads * rows * padded * LANES,
            bytes_accessed=16 * rows * plan.wide,
            transcendentals=plan.heads * rows * padded,
        ),
        name="attend",
    )(key_labels, query_labels, query, key, value, mixed_grad)


def weight_grad_kernel(
    plan, tables, normed_ref, grad_ref, mixed_ref, query_grad_ref, key_grad_ref, value_grad_ref, *rest
):
    sets = len(tables)
    place_refs, rest = rest[:sets], rest[sets:]
    outs, rest = rest[: 2 * sets], rest[2 * sets :]
    held = rest[:2]
    sems = rest[2]
    split, wide = plan.start, plan.wide
    depth = normed_ref.shape[0]
    step = depth // 4
    for at in range(4):
        here = slice(at * step, (at + 1) * step)
        for pair, (first, second, second_left) in enumerate(
            ((query_grad_ref, mixed_ref, grad_ref), (key_grad_ref, value_grad_ref, normed_ref))
        ):
            left = nn_dot(normed_ref[here, :], first[...])
            right = nn_dot(second_left[here, :], second[...])
            seam = left[:, split:wide] + right[:, : wide - split]
            held[pair][here, :split] = left[:, :split].astype(bf16)
            held[pair][here, split:wide] = seam.astype(bf16)
            held[pair][here, wide:] = right[:, wide - split :].astype(bf16)
    copies = []
    for number, (count, rows) in enumerate(tables):
        for pair in range(2):
            for at in range(count):
                first = place_refs[number][at] * rows
                if rows % 16 == 0:
                    first = pl.multiple_of(first, 16)
                copy = pltpu.make_async_copy(
                    held[pair].at[pl.ds(first, rows)], outs[2 * number + pair].at[at], sems.at[len(copies)]
                )
                copy.start()
                copies.append(copy)
    for copy in copies:
        copy.wait()


def weight_grads(plan, normed_turned, grad_turned, mixed, query_grad, key_grad, value_grad, places, rows):
    depth, padded = normed_turned.shape
    tables = tuple((place.shape[0], rows) for place in places)
    out = [jax.ShapeDtypeStruct((count, rows, plan.both), bf16) for count, rows in tables for _ in range(2)]
    return pl.pallas_call(
        functools.partial(weight_grad_kernel, plan, tables),
        out_shape=out,
        in_specs=[WHOLE] * 6 + [SCALARS] * len(places),
        out_specs=[ANYWHERE] * len(out),
        scratch_shapes=[
            pltpu.VMEM((depth, plan.both), bf16),
            pltpu.VMEM((depth, plan.both), bf16),
            pltpu.SemaphoreType.DMA((2 * sum(count for count, _ in tables),)),
        ],
        compiler_params=BIG,
        cost_estimate=pl.CostEstimate(
            flops=8 * depth * padded * plan.wide, bytes_accessed=4 * depth * plan.both, transcendentals=0
        ),
        name="weight_grads",
    )(normed_turned, grad_turned, mixed, query_grad, key_grad, value_grad, *places)


def finish_kernel(plan, sides, *rest):
    weights, rest = rest[:4], rest[4:]
    mixed, query, key, value = (rest[2 * at : 2 * at + 2] for at in range(4))
    normed_ref, inverse_ref, gain_ref, out_ref, part_ref, gain_part_ref, bias_part_ref, held = rest[8:]
    rows = normed_ref.shape[0]
    side = pl.program_id(0)
    left, right = slice(0, plan.wide), slice(plan.start, plan.both)
    out_sum = jnp.zeros(out_ref.shape[1:], f32)
    grad_sum = jnp.zeros(out_ref.shape[1:], f32)
    for chunk in range(2):
        qo_ref, kv_ref = weights[2 * chunk], weights[2 * chunk + 1]
        out_sum += nt_dot(mixed[chunk][:rows, :], qo_ref[:, right])
        grad_sum += nt_dot(query[chunk][:rows, :], qo_ref[:, left])
        grad_sum += nt_dot(key[chunk][:rows, :], kv_ref[:, left])
        grad_sum += nt_dot(value[chunk][:rows, :], kv_ref[:, right])
    out_ref[0] = out_sum.astype(bf16)
    held[side] = grad_sum

    @pl.when(side == sides - 1)
    def _():
        width = held.shape[2]
        total = sides * width
        mean_a = jnp.zeros((rows, 1), f32)
        mean_b = jnp.zeros((rows, 1), f32)
        for at in range(sides):
            here = slice(at * width, (at + 1) * width)
            grad = held[at]
            normed = normed_ref[:, here]
            gain_part_ref[:, here] = jnp.sum(grad * normed, axis=0, keepdims=True)
            bias_part_ref[:, here] = jnp.sum(grad, axis=0, keepdims=True)
            scaled = grad * gain_ref[:, here]
            mean_a += jnp.sum(scaled, axis=1, keepdims=True)
            mean_b += jnp.sum(scaled * normed, axis=1, keepdims=True)
        mean_a = mean_a / total
        mean_b = mean_b / total
        for at in range(sides):
            here = slice(at * width, (at + 1) * width)
            scaled = held[at] * gain_ref[:, here]
            part = inverse_ref[...] * (scaled - mean_a - normed_ref[:, here] * mean_b)
            part_ref[at] = part.astype(bf16)


def finish(plan, weights, mixed, query_grads, key_grads, value_grads, normed, inverse, gain, sides):
    rows, depth = normed.shape
    width = depth // sides
    return pl.pallas_call(
        functools.partial(finish_kernel, plan, sides),
        grid=(sides,),
        out_shape=[
            jax.ShapeDtypeStruct((sides, rows, width), bf16),
            jax.ShapeDtypeStruct((sides, rows, width), bf16),
            jax.ShapeDtypeStruct((1, depth), f32),
            jax.ShapeDtypeStruct((1, depth), f32),
        ],
        in_specs=[pl.BlockSpec((width, plan.both), lambda side: (side, 0))] * 4 + [WHOLE] * 11,
        out_specs=[pl.BlockSpec((1, rows, width), lambda side: (side, 0, 0))] + [WHOLE] * 3,
        scratch_shapes=[pltpu.VMEM((sides, rows, width), f32)],
        compiler_params=BIG,
        cost_estimate=pl.CostEstimate(
            flops=16 * rows * depth * plan.wide, bytes_accessed=8 * depth * plan.both, transcendentals=0
        ),
        name="finish",
    )(*weights, *mixed, *query_grads, *key_grads, *value_grads, normed, inverse, gain[None, :])


def adam_kernel(plan, scale, *refs):
    grads, (master, first, second), outs = refs[:4], refs[4:7], refs[7:]
    half = plan.kind
    for kind, (pair, side) in enumerate(((0, 0), (1, 0), (1, 1), (0, 1))):
        parts = [grads[2 * chunk + pair][:, side * half : (side + 1) * half] for chunk in range(2)]
        gradient = jnp.concatenate(parts, axis=1) * scale
        new = adam_update(master[:, kind, :], first[:, kind, :], second[:, kind, :], gradient, decay_rate)
        for out, value in zip(outs, new):
            out[:, kind, :] = value


def adam(plan, scale, grads, master, first, second):
    return pl.pallas_call(
        functools.partial(adam_kernel, plan, scale),
        out_shape=[jax.ShapeDtypeStruct(master.shape, f32)] * 3,
        in_specs=[WHOLE] * 7,
        out_specs=[WHOLE] * 3,
        compiler_params=BIG,
        name="adam",
    )(*grads, master, first, second)


def ring_of(chips):
    return list(range(0, chips, 2)) + list(range(chips - 1, 0, -2))


class Ring:
    def __init__(self, devices):
        self.chips = devices // 2
        walk = ring_of(self.chips)
        self.moves, self.swap = [], [(device, device ^ 1) for device in range(devices)]
        for at, chip in enumerate(walk):
            self.moves.append((2 * chip, 2 * walk[(at + 1) % self.chips]))
            self.moves.append((2 * chip + 1, 2 * walk[(at - 1) % self.chips] + 1))
        place = {chip: at for at, chip in enumerate(walk)}
        self.arrive, self.mine, self.other = [], [], []
        for device in range(devices):
            at, core = place[device // 2], device % 2

            def come(core, step):
                return 2 * walk[(at + (step if core else -step)) % self.chips] + core

            def leave(core, step):
                return 2 * walk[(at + (1 + step if core else -1 - step)) % self.chips] + core

            steps = range(self.chips)
            self.arrive.append([come(c, s) for s in steps for c in (core, 1 - core)])
            self.mine.append([leave(core, s) for s in steps])
            self.other.append([leave(1 - core, s) for s in steps])

    def row(self, table):
        return jnp.asarray(table, jnp.int32)[lax.axis_index("dp")]

    def gather(self, block):
        blocks = []
        for step in range(self.chips):
            blocks += [block, lax.ppermute(block, "dp", self.swap)]
            if step + 1 < self.chips:
                block = lax.ppermute(block, "dp", self.moves)
        return blocks

    def reduce(self, mine, other):
        near = lax.ppermute(other, "dp", self.swap)
        total = mine[0].astype(f32) + near[0].astype(f32)
        for step in range(1, self.chips):
            total = lax.ppermute(total.astype(bf16), "dp", self.moves).astype(f32)
            total = total + (mine[step].astype(f32) + near[step].astype(f32))
        return total


def sum_over_all(values, axes):
    for axis in axes:
        size = lax.axis_size(axis)
        if size & (size - 1):
            values = lax.psum(values, axis)
            continue
        reach = 1
        while reach < size:
            swap = [(at, at ^ reach) for at in range(size)]
            values = values + lax.ppermute(values, axis, swap)
            reach *= 2
    return values


def shards(
    tokens,
    cotangent,
    master,
    moment_one,
    moment_two,
    ln_gain,
    ln_bias,
    norm_moment_one,
    norm_moment_two,
    image_count,
    tokens_per_image,
):
    groups = lax.axis_size("dp")
    sides = lax.axis_size("mp")
    side = lax.axis_index("mp")
    plan = Plan(master.shape[2])
    shard_rows = master.shape[0]
    depth = shard_rows * groups
    rows, width = tokens.shape
    padded = round_up(rows, LANES)
    around = shard_rows % 16 == 0 and groups % 4 == 0
    swap_sides = [(at, at ^ 1) for at in range(sides)]

    packed = pack(plan, master)
    if around:
        ring = Ring(groups)
        blocks = [ring.gather(block) for block in packed]
        places = ring.row(ring.arrive)
        leave = [ring.row(ring.mine), ring.row(ring.other)]
        leave_rows = shard_rows
    else:
        blocks = [[lax.all_gather(block, "dp", axis=0, tiled=True)] for block in packed]
        places = jnp.zeros((1,), jnp.int32)
        leave = [places]
        leave_rows = depth

    other_tokens = lax.ppermute(tokens, "mp", swap_sides)
    other_cot = lax.ppermute(cotangent, "mp", swap_sides)

    def in_order(here, there):
        return jnp.concatenate([jnp.where(side == 0, here, there), jnp.where(side == 0, there, here)], axis=1)

    normed, inverse, normed_low = layer_norm(in_order(tokens, other_tokens), ln_gain, ln_bias)
    spots = jnp.arange(padded, dtype=jnp.int32)
    live = spots < image_count[0] * tokens_per_image[0]
    labels = jnp.where(live, spots // tokens_per_image[0], jnp.int32(-1))
    live_column = live[:rows, None]
    key_labels = labels[:rows, None]
    query_labels = jnp.where(spots < rows, labels, jnp.int32(-2))[None, :]
    grad_rows = jnp.where(live_column, in_order(cotangent, other_cot), jnp.zeros((), bf16))
    fill = ((0, padded - rows), (0, 0))
    normed_turned = jnp.pad(normed_low, fill).T
    grad_turned = jnp.pad(grad_rows, fill).T

    weights, mixed, query_grads, key_grads, value_grads, totals = [], [], [], [], [], []
    for chunk in range(2):
        query, key, value, mixed_grad, *full = project(
            plan, places, normed_low, grad_rows, blocks[2 * chunk] + blocks[2 * chunk + 1]
        )
        weights += full
        grads = attend(plan, key_labels, query_labels, query, key, value, mixed_grad)
        for held, one in zip((mixed, query_grads, key_grads, value_grads), grads):
            held.append(one)
        parts = weight_grads(plan, normed_turned, grad_turned, *grads, leave, leave_rows)
        for pair in range(2):
            if around:
                totals.append(ring.reduce(parts[pair], parts[2 + pair]))
            else:
                total = lax.psum_scatter(parts[pair][0], "dp", scatter_dimension=0, tiled=True)
                totals.append(total.astype(f32))

    out_parts, input_parts, gain_part, bias_part = finish(
        plan, weights, mixed, query_grads, key_grads, value_grads, normed, inverse, ln_gain, sides
    )

    def across(parts):
        away = lax.ppermute(parts[1 - side], "mp", swap_sides)
        return parts[side].astype(f32) + away.astype(f32)

    block_out = (tokens.astype(f32) + across(out_parts)).astype(bf16)
    grad_local = jnp.where(live_column, cotangent, jnp.zeros((), bf16))
    input_grad = (grad_local.astype(f32) + across(input_parts)).astype(bf16)

    norm_param_grad = sum_over_all(jnp.concatenate([gain_part, bias_part]), ("dp", "mp")) / groups
    new_norm, new_norm_moment_one, new_norm_moment_two = adam_update(
        jnp.stack([ln_gain, ln_bias]), norm_moment_one, norm_moment_two, norm_param_grad, 0.0
    )
    new_master, new_moment_one, new_moment_two = adam(
        plan, 1.0 / groups, totals, master, moment_one, moment_two
    )
    return (
        block_out,
        input_grad,
        new_master,
        new_moment_one,
        new_moment_two,
        new_norm[0],
        new_norm[1],
        new_norm_moment_one,
        new_norm_moment_two,
    )


def solution(mesh):
    rows = P("dp", "mp")
    cube = P("dp", None, "mp")
    return jax.shard_map(
        shards,
        mesh=mesh,
        in_specs=(rows, rows, cube, cube, cube, P(), P(), P(), P(), P("dp"), P("dp")),
        out_specs=(rows, rows, cube, cube, cube, P(), P(), P(), P()),
        check_vma=False,
    )
```

time: 548 us -> 295 us (0.54)
  waiting for transfers between devices: 353 us -> 62 us
  starting transfers between devices: 0.62 us -> 91.9 us
  Pallas kernels: 0 us -> 84.7 us
  matrix products: 68.8 us -> 0 us
  blocking collectives: 39.9 us -> 0 us
  between operations: 16 us -> 3.08 us
  local copies, waits for them, and re-layouts: 39.9 us -> 30.6 us
  other arithmetic: 24.5 us -> 18.1 us
    reduce_scatter x1 -> x0, waiting for transfers between devices: 214 us -> none  [shards(): lax.psum_scatter(full_grad, 'dp', scatter_dimension=0, tiled=True)]
    all_gather x3 -> x0, waiting for transfers between devices: 137 us -> none  [the longest x1 102 us: shards(): lax.all_gather(master.astype(jnp.bfloat16), 'dp', axis=0, tiled=True)]
    ppermute x0 -> x101, starting transfers between devices: none -> 91.9 us  [the longest x28 43.3 us: gather(): block = lax.ppermute(block, 'dp', self.moves)]
    pallas_call x0 -> x9, Pallas kernels: none -> 84.7 us  [the longest x1 24.2 us: finish(): pl.pallas_call(functools.partial(finish_kernel, plan, sides), grid=(sides...]
    dot_general x12 -> x0, matrix products: 68.8 us -> none  [the longest x1 13.2 us: shards(): jnp.einsum('hqk,khd->qhd', score_grad, key_rows, preferred_element_type=j...]
    ppermute x0 -> x101, waiting for transfers between devices: none -> 62 us  [the longest x28 27.1 us: reduce(): total = lax.ppermute(total.astype(bf16), 'dp', self.moves).astype(f32)]
    psum x1 -> x0, blocking collectives: 39.9 us -> none  [shards(): gain_sum, bias_sum = lax.psum((gain_part, bias_part), ('dp', 'mp'))]
    unnamed x42 -> x112, local copies, waits for them, and re-layouts: 19.4 us -> 4.88 us
  transfers between devices with their start and end apart: 6 -> 101, of which waited for: 4 -> 44; matrix products, arithmetic and copies ran while one was open for 18% -> 15% of each run, Pallas kernels for 0% -> 12%
where the time goes in v1:
time: 295 us; the launch traced here: 290 us
  starting transfers between devices  91.9 us (31%)
  Pallas kernels  84.7 us (29%)
  waiting for transfers between devices  62 us (21%)
  local copies, waits for them, and re-layouts  30.6 us (10%)
  other arithmetic  18.1 us (6%)
  between operations  3.08 us (1%)
    ppermute x28, starting transfers between devices, gather(): block = lax.ppermute(block, 'dp', self.moves)  43.3 us
    ppermute x28, starting transfers between devices, reduce(): total = lax.ppermute(total.astype(bf16), 'dp', self.moves).astype(f32)  31.9 us
    ppermute x28, waiting for transfers between devices, reduce(): total = lax.ppermute(total.astype(bf16), 'dp', self.moves).astype(f32)  27.1 us
    pallas_call x1, Pallas kernels, finish(): pl.pallas_call(functools.partial(finish_kernel, plan, sides), grid=(sides...  24.2 us
    pallas_call x2, Pallas kernels, weight_grads(): pl.pallas_call(functools.partial(weight_grad_kernel, plan, tables), out_s...  18.2 us
    pallas_call x2, Pallas kernels, project(): pl.pallas_call(functools.partial(project_kernel, plan, count), out_shape=...  17.3 us
    pallas_call x2, Pallas kernels, attend(): pl.pallas_call(functools.partial(attend_kernel, plan), out_shape=[out] *...  13.8 us
    ppermute x2, waiting for transfers between devices, across(): away = lax.ppermute(parts[1 - side], 'mp', swap_sides)  13.5 us
  transfers between devices with their start and end apart: 101, of which 44 were waited for; matrix products, arithmetic and copies ran while one was open for 15% of the time, Pallas kernels for 12%

profile of v1, /device:TPU:0, one launch (start us, length us, event | category | flops | bytes accessed | tf_op | source)
XLA Modules:
  0.0 290.4 jit_solution(6993184840031112459)
XLA Ops:
  0.7 2.7 pack.1
  3.3 3.0 %collective-permute-start.3 = (bf16[112,896]{1,0:T(8,128)(2,1)}, bf16[112,896]{1,0:T(8,128)(2,1)}, u32[]{:S(2)}, u32[]{:S(2)}) collective-permute-start(bf16[112,896]{1,0:T(8,128)(2,1)} %get-tuple-element.48.rest_0_), channel_id=1, source_target_pairs={{0,8},{2,6},{8,16},{10,2},{16,24},{18,10},{24,28},{26,18},{28,20},... | collective-permute-start | bytes 602120 | tf_op jit(solution)/shard_map/ppermute | solution.py:413
  6.4 1.6 collective-permute-start.18
  7.9 1.6 collective-permute-start.33
  10.3 2.1 collective-permute-start
  12.4 2.1 collective-permute-start.1
  14.5 1.6 collective-permute-start.48
  16.1 1.6 collective-permute-start.5
  17.7 2.8 collective-permute-done.48.rest_18_
  20.5 1.6 collective-permute-start.20
  27.2 1.6 collective-permute-start.35
  28.9 1.5 collective-permute-start.50
  33.1 1.6 collective-permute-start.7
  35.2 1.6 collective-permute-start.22
  36.9 7.7 %collective-permute-done.1 = bf16[400,896]{1,0:T(8,128)(2,1)} collective-permute-done((bf16[400,896]{1,0:T(8,128)(2,1)S(1)}, bf16[400,896]{1,0:T(8,128)(2,1)}, u32[]{:S(2)}, u32[]{:S(2)}) %collective-permute-start.1) | collective-permute-done | bytes 716832 | tf_op jit(solution)/shard_map/ppermute | solution.py:477
  46.6 1.6 copy.49
  48.2 2.2 copy.53
  50.4 1.8 collective-permute-start.37
  52.4 1.5 collective-permute-start.52
  53.9 1.6 collective-permute-start.9
  57.5 1.5 collective-permute-start.24
  60.7 1.8 collective-permute-start.54
  63.5 1.5 collective-permute-start.11
  65.6 1.5 collective-permute-start.26
  69.9 1.5 collective-permute-start.56
  72.1 1.5 collective-permute-start.13
  74.3 1.5 collective-permute-start.28
  79.9 3.8 %fusion = (f32[400,1792]{0,1:T(8,128)}, bf16[400,1792]{0,1:T(8,128)(2,1)S(1)}) fusion(f32[400]{0:T(512)S(1)} %add_rsqrt_fusion, f32[400]{0:T(512)S(1)} %broadcast_multiply_fusion, bf16[400,896]{0,1:T(8,128)(2,1)S(1)} %get-tuple-element.100, bf16[400,896]{0,1:T(8,128)(2,1)S(1)} %get-tuple-element.101, f32[1792]{0:T(1024)S(1)} %copy-done.12, f32[1792]{0:T(1024)S(1)} %copy-done.13), kind=kLoop, calls=%fused_computation.2 | loop fusion | flops 6451200 | bytes 5751936 | tf_op jit(solution)/shard_map/mul | solution.py:47
  84.6 1.6 collective-permute-start.15
  86.2 1.5 collective-permute-start.45
  88.3 1.6 maximum_select_fusion
  90.7 3.7 %copy.57.grad_ref = bf16[400,1792]{1,0:T(8,128)(2,1)} copy(bf16[400,1792]{0,1:T(8,128)(2,1)} %maximum_select_fusion) | data formatting | bytes 2867200 | tf_op jit(solution)/shard_map/jit(_where)/select_n | solution.py:489
  94.5 5.0 %copy.62.rest_12_ = f32[400,1792]{1,0:T(8,128)} copy(f32[400,1792]{0,1:T(8,128)} %get-tuple-element.92) | data formatting | bytes 5734400 | tf_op jit(solution)/shard_map/mul | solution.py:47
  99.4 2.3 copy.56.normed_ref
  104.4 3.0 %pad_bitcast_fusion.grad_ref = bf16[1792,512]{1,0:T(8,128)(2,1)} fusion(bf16[400,1792]{0,1:T(8,128)(2,1)} %maximum_select_fusion), kind=kLoop, calls=%fused_computation.8 | loop fusion | bytes 3268608 | tf_op jit(solution)/shard_map/transpose | solution.py:492
  110.2 8.6 %project.3 = (bf16[400,512]{1,0:T(8,128)(2,1)}, bf16[400,512]{1,0:T(8,128)(2,1)}, bf16[400,512]{1,0:T(8,128)(2,1)}, bf16[400,512]{1,0:T(8,128)(2,1)}, bf16[1792,...) custom-call(s32[16]{0:T(128)} %fusion.37.place_ref, bf16[400,1792]{1,0:T(8,128)(2,1)} %copy.56.normed_ref, ...), custom_call_target="tpu_custom_call" | custom-call | flops 2936012800 | bytes 12845056 | tf_op jit(solution)/shard_map/project/pallas_call | solution.py:138
  118.9 6.9 %attend.3 = (bf16[512,512]{1,0:T(8,128)(2,1)}, bf16[512,512]{1,0:T(8,128)(2,1)}, bf16[512,512]{1,0:T(8,128)(2,1)}, bf16[512,512]{1,0:T(8,128)(2,1)}) custom-call(s32[400,1]{1,0:T(8,128)} %copy.60.key_label_ref, s32[1,512]{1,0:T(1,128)} %compare_select_fusion.1.query_label_ref, bf16[400,512]{1,0:T(8,128)(2,1)} %get-tuple-element.61.query_ref, ...), custom_call_target="tpu_custom_call" | custom-call | flops 1677721600 | bytes 3276800 | tf_op jit(solution)/shard_map/attend/pallas_call | solution.py:209
  127.4 8.7 %project.2 = (bf16[400,512]{1,0:T(8,128)(2,1)}, bf16[400,512]{1,0:T(8,128)(2,1)}, bf16[400,512]{1,0:T(8,128)(2,1)}, bf16[400,512]{1,0:T(8,128)(2,1)}, bf16[1792,...) custom-call(s32[16]{0:T(128)} %fusion.37.place_ref, bf16[400,1792]{1,0:T(8,128)(2,1)} %copy.56.normed_ref, ...), custom_call_target="tpu_custom_call" | custom-call | flops 2936012800 | bytes 12845056 | tf_op jit(solution)/shard_map/project/pallas_call | solution.py:138
  136.0 6.8 %attend.2 = (bf16[512,512]{1,0:T(8,128)(2,1)}, bf16[512,512]{1,0:T(8,128)(2,1)}, bf16[512,512]{1,0:T(8,128)(2,1)}, bf16[512,512]{1,0:T(8,128)(2,1)}) custom-call(s32[400,1]{1,0:T(8,128)} %copy.60.key_label_ref, s32[1,512]{1,0:T(1,128)} %compare_select_fusion.1.query_label_ref, bf16[400,512]{1,0:T(8,128)(2,1)} %get-tuple-element.56.query_ref, ...), custom_call_target="tpu_custom_call" | custom-call | flops 1677721600 | bytes 3276800 | tf_op jit(solution)/shard_map/attend/pallas_call | solution.py:209
  142.9 24.2 %finish.1 = (bf16[2,400,896]{2,1,0:T(8,128)(2,1)}, bf16[2,400,896]{2,1,0:T(8,128)(2,1)}, f32[1,1792]{1,0:T(1,128)}, f32[1,1792]{1,0:T(1,128)}) custom-call(bf16[1792,896]{1,0:T(8,128)(2,1)} %get-tuple-element.50.rest_0_, bf16[1792,896]{1,0:T(8,128)(2,1)} %get-tuple-element.51.rest_1_, bf16[1792,896]{1,0:T(8,128)(2,1)} %get-tuple-element.54.rest_2_, ...), custom_call_target="tpu_custom_call" | custom-call | flops 5872025600 | bytes 12845056 | tf_op jit(solution)/shard_map/finish/pallas_call | solution.py:335
  171.8 1.5 collective-permute-start.62
  174.0 9.1 %weight_grads.2 = (bf16[8,112,896]{2,1,0:T(8,128)(2,1)}, bf16[8,112,896]{2,1,0:T(8,128)(2,1)}, bf16[8,112,896]{2,1,0:T(8,128)(2,1)}, bf16[8,112,896]{2,1,0:T(8,128)(2,1)}) custom-call(bf16[1792,512]{1,0:T(8,128)(2,1)} %pad_bitcast_fusion.1.normed_ref, bf16[1792,512]{1,0:T(8,128)(2,1)} %pad_bitcast_fusion.grad_ref, ...), custom_call_target="tpu_custom_call" | custom-call | flops 3758096384 | bytes 6422528 | tf_op jit(solution)/shard_map/weight_grads/pallas_call | solution.py:272
  183.7 1.6 collective-permute-start.99
  185.3 9.1 %weight_grads.3 = (bf16[8,112,896]{2,1,0:T(8,128)(2,1)}, bf16[8,112,896]{2,1,0:T(8,128)(2,1)}, bf16[8,112,896]{2,1,0:T(8,128)(2,1)}, bf16[8,112,896]{2,1,0:T(8,128)(2,1)}) custom-call(bf16[1792,512]{1,0:T(8,128)(2,1)} %pad_bitcast_fusion.1.normed_ref, bf16[1792,512]{1,0:T(8,128)(2,1)} %pad_bitcast_fusion.grad_ref, ...), custom_call_target="tpu_custom_call" | custom-call | flops 3758096384 | bytes 6422528 | tf_op jit(solution)/shard_map/weight_grads/pallas_call | solution.py:272
  196.0 2.3 collective-permute-done.100
  202.1 13.5 %collective-permute-done.63 = bf16[400,896]{1,0:T(8,128)(2,1)S(1)} collective-permute-done((bf16[400,896]{1,0:T(8,128)(2,1)S(1)}, bf16[400,896]{1,0:T(8,128)(2,1)S(1)}, u32[]{:S(2)}, u32[]{:S(2)}) %collective-permute-start.63) | collective-permute-done | bytes 716832 | tf_op jit(solution)/shard_map/ppermute | solution.py:516
  219.1 1.5 collective-permute-start.81
  281.6 8.6 %adam.1 = (f32[112,4,896]{2,1,0:T(4,128)}, f32[112,4,896]{2,1,0:T(4,128)}, f32[112,4,896]{2,1,0:T(4,128)}) custom-call(f32[112,896]{1,0:T(8,128)} %bitcast_add_fusion.21.refs_0_, f32[112,896]{1,0:T(8,128)} %bitcast_add_fusion.14.refs_1_, f32[112,896]{1,0:T(8,128)} %bitcast_add_fusion.7.refs_2_, f32[112,896]{1,0:T(8,128)} %bitcast_add_fusion.refs_3_, ...), custom_call_target="tpu_custom_call" | custom-call | tf_op jit(solution)/shard_map/adam/pallas_call | solution.py:367
  (341 shorter events, 107.9 us)
Async XLA Ops:
  10.3 24.9 %collective-permute-start = (bf16[400,896]{1,0:T(8,128)(2,1)S(1)}, bf16[400,896]{1,0:T(8,128)(2,1)}, u32[]{:S(2)}, u32[]{:S(2)}) collective-permute-start(bf16[400,896]{1,0:T(8,128)(2,1)S(1)} %copy-done), channel_id=1, source_target_pairs={{0,1},{1,0},{2,3},{3,2},{4,5},{5,4},{6,7},{7,6},{8,9},{9,8},{10,11... | collective-permute-start | bytes 2150408 | tf_op jit(solution)/shard_map/ppermute | solution.py:476
  12.4 32.2 %collective-permute-start.1 = (bf16[400,896]{1,0:T(8,128)(2,1)S(1)}, bf16[400,896]{1,0:T(8,128)(2,1)}, u32[]{:S(2)}, u32[]{:S(2)}) collective-permute-start(bf16[400,896]{1,0:T(8,128)(2,1)S(1)} %copy-done.1), channel_id=1, source_target_pairs={{0,1},{1,0},{2,3},{3,2},{4,5},{5,4},{6,7},{7,6},{8,9},{9,8},{10,11... | collective-permute-start | bytes 2150408 | tf_op jit(solution)/shard_map/ppermute | solution.py:477
  33.1 17.3 %collective-permute-start.49 = (bf16[112,896]{1,0:T(8,128)(2,1)}, bf16[112,896]{1,0:T(8,128)(2,1)}, u32[]{:S(2)}, u32[]{:S(2)}) collective-permute-start(bf16[112,896]{1,0:T(8,128)(2,1)} %collective-permute-done.48.rest_18_), channel_id=1, source_target_pairs={{0,2},{2,0},{4,6},{6,4},{8,10},{10,8},{12,14},{14,12},{16,18},{18,... | collective-permute-start | bytes 602120 | tf_op jit(solution)/shard_map/ppermute | solution.py:411
  33.1 19.1 %collective-permute-start.7 = (bf16[112,896]{1,0:T(8,128)(2,1)}, bf16[112,896]{1,0:T(8,128)(2,1)}, u32[]{:S(2)}, u32[]{:S(2)}) collective-permute-start(bf16[112,896]{1,0:T(8,128)(2,1)} %collective-permute-done.5.rest_4_), channel_id=1, source_target_pairs={{0,8},{2,6},{8,16},{10,2},{16,24},{18,10},{24,28},{26,18},{28,20},... | collective-permute-start | bytes 602120 | tf_op jit(solution)/shard_map/ppermute | solution.py:413
  35.2 17.1 %collective-permute-start.6 = (bf16[112,896]{1,0:T(8,128)(2,1)}, bf16[112,896]{1,0:T(8,128)(2,1)}, u32[]{:S(2)}, u32[]{:S(2)}) collective-permute-start(bf16[112,896]{1,0:T(8,128)(2,1)} %collective-permute-done.5.rest_4_), channel_id=1, source_target_pairs={{0,2},{2,0},{4,6},{6,4},{8,10},{10,8},{12,14},{14,12},{16,18},{18,... | collective-permute-start | bytes 602120 | tf_op jit(solution)/shard_map/ppermute | solution.py:411
  35.2 18.6 %collective-permute-start.22 = (bf16[112,896]{1,0:T(8,128)(2,1)}, bf16[112,896]{1,0:T(8,128)(2,1)}, u32[]{:S(2)}, u32[]{:S(2)}) collective-permute-start(bf16[112,896]{1,0:T(8,128)(2,1)} %collective-permute-done.20.rest_20_), channel_id=1, source_target_pairs={{0,8},{2,6},{8,16},{10,2},{16,24},{18,10},{24,28},{26,18},{28,20},... | collective-permute-start | bytes 602120 | tf_op jit(solution)/shard_map/ppermute | solution.py:413
  44.6 9.3 %collective-permute-start.21 = (bf16[112,896]{1,0:T(8,128)(2,1)}, bf16[112,896]{1,0:T(8,128)(2,1)}, u32[]{:S(2)}, u32[]{:S(2)}) collective-permute-start(bf16[112,896]{1,0:T(8,128)(2,1)} %collective-permute-done.20.rest_20_), channel_id=1, source_target_pairs={{0,2},{2,0},{4,6},{6,4},{8,10},{10,8},{12,14},{14,12},{16,18},{18,... | collective-permute-start | bytes 602120 | tf_op jit(solution)/shard_map/ppermute | solution.py:411
  72.1 11.7 %collective-permute-start.13 = (bf16[112,896]{1,0:T(8,128)(2,1)S(1)}, bf16[112,896]{1,0:T(8,128)(2,1)}, u32[]{:S(2)}, u32[]{:S(2)}) collective-permute-start(bf16[112,896]{1,0:T(8,128)(2,1)S(1)} %collective-permute-done.11.rest_10_), channel_id=1, source_target_pairs={{0,8},{2,6},{8,16},{10,2},{16,24},{18,10},{24,28},{26,18},{28,20},... | collective-permute-start | bytes 602120 | tf_op jit(solution)/shard_map/ppermute | solution.py:413
  74.3 9.6 %collective-permute-start.12 = (bf16[112,896]{1,0:T(8,128)(2,1)S(1)}, bf16[112,896]{1,0:T(8,128)(2,1)S(1)}, u32[]{:S(2)}, u32[]{:S(2)}) collective-permute-start(bf16[112,896]{1,0:T(8,128)(2,1)S(1)} %collective-permute-done.11.rest_10_), channel_id=1, source_target_pairs={{0,2},{2,0},{4,6},{6,4},{8,10},{10,8},{12,14},{14,12},{16,18},{18,... | collective-permute-start | bytes 602120 | tf_op jit(solution)/shard_map/ppermute | solution.py:411
  74.3 10.1 %collective-permute-start.28 = (bf16[112,896]{1,0:T(8,128)(2,1)S(1)}, bf16[112,896]{1,0:T(8,128)(2,1)S(1)}, u32[]{:S(2)}, u32[]{:S(2)}) collective-permute-start(bf16[112,896]{1,0:T(8,128)(2,1)S(1)} %collective-permute-done.26.rest_26_), channel_id=1, source_target_pairs={{0,8},{2,6},{8,16},{10,2},{16,24},{18,10},{24,28},{26,18},{28,20},... | collective-permute-start | bytes 602120 | tf_op jit(solution)/shard_map/ppermute | solution.py:413
  76.4 9.7 %collective-permute-start.43 = (bf16[112,896]{1,0:T(8,128)(2,1)}, bf16[112,896]{1,0:T(8,128)(2,1)}, u32[]{:S(2)}, u32[]{:S(2)}) collective-permute-start(bf16[112,896]{1,0:T(8,128)(2,1)} %collective-permute-done.41.rest_10_), channel_id=1, source_target_pairs={{0,8},{2,6},{8,16},{10,2},{16,24},{18,10},{24,28},{26,18},{28,20},... | collective-permute-start | bytes 602120 | tf_op jit(solution)/shard_map/ppermute | solution.py:413
  78.7 9.0 %collective-permute-start.58 = (bf16[112,896]{1,0:T(8,128)(2,1)}, bf16[112,896]{1,0:T(8,128)(2,1)}, u32[]{:S(2)}, u32[]{:S(2)}) collective-permute-start(bf16[112,896]{1,0:T(8,128)(2,1)} %collective-permute-done.56.rest_26_), channel_id=1, source_target_pairs={{0,8},{2,6},{8,16},{10,2},{16,24},{18,10},{24,28},{26,18},{28,20},... | collective-permute-start | bytes 602120 | tf_op jit(solution)/shard_map/ppermute | solution.py:413
  83.8 17.9 %collective-permute-start.42 = (bf16[112,896]{1,0:T(8,128)(2,1)}, bf16[112,896]{1,0:T(8,128)(2,1)}, u32[]{:S(2)}, u32[]{:S(2)}) collective-permute-start(bf16[112,896]{1,0:T(8,128)(2,1)} %collective-permute-done.41.rest_10_), channel_id=1, source_target_pairs={{0,2},{2,0},{4,6},{6,4},{8,10},{10,8},{12,14},{14,12},{16,18},{18,... | collective-permute-start | bytes 602120 | tf_op jit(solution)/shard_map/ppermute | solution.py:411
  83.9 17.9 %collective-permute-start.57 = (bf16[112,896]{1,0:T(8,128)(2,1)}, bf16[112,896]{1,0:T(8,128)(2,1)S(1)}, u32[]{:S(2)}, u32[]{:S(2)}) collective-permute-start(bf16[112,896]{1,0:T(8,128)(2,1)} %collective-permute-done.56.rest_26_), channel_id=1, source_target_pairs={{0,2},{2,0},{4,6},{6,4},{8,10},{10,8},{12,14},{14,12},{16,18},{18,... | collective-permute-start | bytes 602120 | tf_op jit(solution)/shard_map/ppermute | solution.py:411
  84.6 17.9 %collective-permute-start.15 = (bf16[112,896]{1,0:T(8,128)(2,1)}, bf16[112,896]{1,0:T(8,128)(2,1)S(1)}, u32[]{:S(2)}, u32[]{:S(2)}) collective-permute-start(bf16[112,896]{1,0:T(8,128)(2,1)} %collective-permute-done.13.rest_12_), channel_id=1, source_target_pairs={{0,8},{2,6},{8,16},{10,2},{16,24},{18,10},{24,28},{26,18},{28,20},... | collective-permute-start | bytes 602120 | tf_op jit(solution)/shard_map/ppermute | solution.py:413
  86.2 17.0 %collective-permute-start.45 = (bf16[112,896]{1,0:T(8,128)(2,1)}, bf16[112,896]{1,0:T(8,128)(2,1)}, u32[]{:S(2)}, u32[]{:S(2)}) collective-permute-start(bf16[112,896]{1,0:T(8,128)(2,1)} %collective-permute-done.43.rest_12_), channel_id=1, source_target_pairs={{0,8},{2,6},{8,16},{10,2},{16,24},{18,10},{24,28},{26,18},{28,20},... | collective-permute-start | bytes 602120 | tf_op jit(solution)/shard_map/ppermute | solution.py:413
  87.6 16.7 %collective-permute-start.60 = (bf16[112,896]{1,0:T(8,128)(2,1)}, bf16[112,896]{1,0:T(8,128)(2,1)}, u32[]{:S(2)}, u32[]{:S(2)}) collective-permute-start(bf16[112,896]{1,0:T(8,128)(2,1)} %collective-permute-done.58.rest_28_), channel_id=1, source_target_pairs={{0,8},{2,6},{8,16},{10,2},{16,24},{18,10},{24,28},{26,18},{28,20},... | collective-permute-start | bytes 602120 | tf_op jit(solution)/shard_map/ppermute | solution.py:413
  108.5 17.4 %collective-permute-start.27 = (bf16[112,896]{1,0:T(8,128)(2,1)S(1)}, bf16[112,896]{1,0:T(8,128)(2,1)S(1)}, u32[]{:S(2)}, u32[]{:S(2)}) collective-permute-start(bf16[112,896]{1,0:T(8,128)(2,1)S(1)} %copy-done.32), channel_id=1, source_target_pairs={{0,2},{2,0},{4,6},{6,4},{8,10},{10,8},{12,14},{14,12},{16,18},{18,... | collective-permute-start | bytes 602120 | tf_op jit(solution)/shard_map/ppermute | solution.py:411
  108.5 17.3 %collective-permute-start.14 = (bf16[112,896]{1,0:T(8,128)(2,1)}, bf16[112,896]{1,0:T(8,128)(2,1)S(1)}, u32[]{:S(2)}, u32[]{:S(2)}) collective-permute-start(bf16[112,896]{1,0:T(8,128)(2,1)} %collective-permute-done.13.rest_12_), channel_id=1, source_target_pairs={{0,2},{2,0},{4,6},{6,4},{8,10},{10,8},{12,14},{14,12},{16,18},{18,... | collective-permute-start | bytes 602120 | tf_op jit(solution)/shard_map/ppermute | solution.py:411
  109.0 16.9 %collective-permute-start.29 = (bf16[112,896]{1,0:T(8,128)(2,1)S(1)}, bf16[112,896]{1,0:T(8,128)(2,1)S(1)}, u32[]{:S(2)}, u32[]{:S(2)}) collective-permute-start(bf16[112,896]{1,0:T(8,128)(2,1)S(1)} %copy-done.40), channel_id=1, source_target_pairs={{0,2},{2,0},{4,6},{6,4},{8,10},{10,8},{12,14},{14,12},{16,18},{18,... | collective-permute-start | bytes 602120 | tf_op jit(solution)/shard_map/ppermute | solution.py:411
  109.1 16.8 %collective-permute-start.16 = (bf16[112,896]{1,0:T(8,128)(2,1)S(1)}, bf16[112,896]{1,0:T(8,128)(2,1)S(1)}, u32[]{:S(2)}, u32[]{:S(2)}) collective-permute-start(bf16[112,896]{1,0:T(8,128)(2,1)S(1)} %collective-permute-done.15.rest_14_), channel_id=1, source_target_pairs={{0,2},{2,0},{4,6},{6,4},{8,10},{10,8},{12,14},{14,12},{16,18},{18,... | collective-permute-start | bytes 602120 | tf_op jit(solution)/shard_map/ppermute | solution.py:411
  109.6 16.3 %collective-permute-start.31 = (bf16[112,896]{1,0:T(8,128)(2,1)S(1)}, bf16[112,896]{1,0:T(8,128)(2,1)S(1)}, u32[]{:S(2)}, u32[]{:S(2)}) collective-permute-start(bf16[112,896]{1,0:T(8,128)(2,1)S(1)} %collective-permute-done.30.rest_30_), channel_id=1, source_target_pairs={{0,2},{2,0},{4,6},{6,4},{8,10},{10,8},{12,14},{14,12},{16,18},{18,... | collective-permute-start | bytes 602120 | tf_op jit(solution)/shard_map/ppermute | solution.py:411
  171.8 27.9 %collective-permute-start.62 = (bf16[400,896]{1,0:T(8,128)(2,1)}, bf16[400,896]{1,0:T(8,128)(2,1)S(1)}, u32[]{:S(2)}, u32[]{:S(2)}) collective-permute-start(bf16[400,896]{1,0:T(8,128)(2,1)} %dynamic-slice_bitcast_fusion.1), channel_id=1, source_target_pairs={{0,1},{1,0},{2,3},{3,2},{4,5},{5,4},{6,7},{7,6},{8,9},{9,8},{10,11... | collective-permute-start | bytes 2150408 | tf_op jit(solution)/shard_map/ppermute | solution.py:516
  173.4 10.3 %collective-permute-start.98 = (f32[2,1792]{1,0:T(2,128)S(1)}, f32[2,1792]{1,0:T(2,128)S(1)}, u32[]{:S(2)}, u32[]{:S(2)}) collective-permute-start(f32[2,1792]{1,0:T(2,128)S(1)} %fusion.41), channel_id=1, source_target_pairs={{0,8},{2,10},{4,12},{6,14},{8,0},{10,2},{12,4},{14,6},{16,24},{18,... | collective-permute-start | bytes 43016 | tf_op jit(solution)/shard_map/ppermute | solution.py:434
  183.1 33.7 %collective-permute-start.64 = (bf16[8,112,896]{2,1,0:T(8,128)(2,1)}, bf16[8,112,896]{2,1,0:T(8,128)(2,1)S(1)}, u32[]{:S(2)}, u32[]{:S(2)}) collective-permute-start(bf16[8,112,896]{2,1,0:T(8,128)(2,1)} %get-tuple-element.75), channel_id=1, source_target_pairs={{0,2},{2,0},{4,6},{6,4},{8,10},{10,8},{12,14},{14,12},{16,18},{18,... | collective-permute-start | bytes 4816904 | tf_op jit(solution)/shard_map/ppermute | solution.py:417
  183.2 34.8 %collective-permute-start.72 = (bf16[8,112,896]{2,1,0:T(8,128)(2,1)}, bf16[8,112,896]{2,1,0:T(8,128)(2,1)S(1)}, u32[]{:S(2)}, u32[]{:S(2)}) collective-permute-start(bf16[8,112,896]{2,1,0:T(8,128)(2,1)} %get-tuple-element.77), channel_id=1, source_target_pairs={{0,2},{2,0},{4,6},{6,4},{8,10},{10,8},{12,14},{14,12},{16,18},{18,... | collective-permute-start | bytes 4816904 | tf_op jit(solution)/shard_map/ppermute | solution.py:417
  183.7 10.8 %collective-permute-start.99 = (f32[2,1792]{1,0:T(2,128)S(1)}, f32[2,1792]{1,0:T(2,128)S(1)}, u32[]{:S(2)}, u32[]{:S(2)}) collective-permute-start(f32[2,1792]{1,0:T(2,128)S(1)} %add.461), channel_id=1, source_target_pairs={{0,16},{2,18},{4,20},{6,22},{8,24},{10,26},{12,28},{14,30},{16,0},... | collective-permute-start | bytes 43016 | tf_op jit(solution)/shard_map/ppermute | solution.py:434
  194.4 24.6 %collective-permute-start.80 = (bf16[8,112,896]{2,1,0:T(8,128)(2,1)}, bf16[8,112,896]{2,1,0:T(8,128)(2,1)S(1)}, u32[]{:S(2)}, u32[]{:S(2)}) collective-permute-start(bf16[8,112,896]{2,1,0:T(8,128)(2,1)} %get-tuple-element.79), channel_id=1, source_target_pairs={{0,2},{2,0},{4,6},{6,4},{8,10},{10,8},{12,14},{14,12},{16,18},{18,... | collective-permute-start | bytes 4816904 | tf_op jit(solution)/shard_map/ppermute | solution.py:417
  198.3 17.3 %collective-permute-start.63 = (bf16[400,896]{1,0:T(8,128)(2,1)S(1)}, bf16[400,896]{1,0:T(8,128)(2,1)S(1)}, u32[]{:S(2)}, u32[]{:S(2)}) collective-permute-start(bf16[400,896]{1,0:T(8,128)(2,1)S(1)} %dynamic-slice_bitcast_fusion), channel_id=1, source_target_pairs={{0,1},{1,0},{2,3},{3,2},{4,5},{5,4},{6,7},{7,6},{8,9},{9,8},{10,11... | collective-permute-start | bytes 2150408 | tf_op jit(solution)/shard_map/ppermute | solution.py:516
  199.7 20.9 %collective-permute-start.88 = (bf16[8,112,896]{2,1,0:T(8,128)(2,1)}, bf16[8,112,896]{2,1,0:T(8,128)(2,1)S(1)}, u32[]{:S(2)}, u32[]{:S(2)}) collective-permute-start(bf16[8,112,896]{2,1,0:T(8,128)(2,1)} %get-tuple-element.81), channel_id=1, source_target_pairs={{0,2},{2,0},{4,6},{6,4},{8,10},{10,8},{12,14},{14,12},{16,18},{18,... | collective-permute-start | bytes 4816904 | tf_op jit(solution)/shard_map/ppermute | solution.py:417
  222.8 8.5 %collective-permute-start.66 = (bf16[112,896]{1,0:T(8,128)(2,1)S(1)}, bf16[112,896]{1,0:T(8,128)(2,1)S(1)}, u32[]{:S(2)}, u32[]{:S(2)}) collective-permute-start(bf16[112,896]{1,0:T(8,128)(2,1)S(1)} %fusion.30), channel_id=1, source_target_pairs={{0,8},{2,6},{8,16},{10,2},{16,24},{18,10},{24,28},{26,18},{28,20},... | collective-permute-start | bytes 602120 | tf_op jit(solution)/shard_map/ppermute | solution.py:420
  224.9 8.5 %collective-permute-start.74 = (bf16[112,896]{1,0:T(8,128)(2,1)S(1)}, bf16[112,896]{1,0:T(8,128)(2,1)S(1)}, u32[]{:S(2)}, u32[]{:S(2)}) collective-permute-start(bf16[112,896]{1,0:T(8,128)(2,1)S(1)} %fusion.24), channel_id=1, source_target_pairs={{0,8},{2,6},{8,16},{10,2},{16,24},{18,10},{24,28},{26,18},{28,20},... | collective-permute-start | bytes 602120 | tf_op jit(solution)/shard_map/ppermute | solution.py:420
  229.2 8.5 %collective-permute-start.90 = (bf16[112,896]{1,0:T(8,128)(2,1)S(1)}, bf16[112,896]{1,0:T(8,128)(2,1)S(1)}, u32[]{:S(2)}, u32[]{:S(2)}) collective-permute-start(bf16[112,896]{1,0:T(8,128)(2,1)S(1)} %fusion.12), channel_id=1, source_target_pairs={{0,8},{2,6},{8,16},{10,2},{16,24},{18,10},{24,28},{26,18},{28,20},... | collective-permute-start | bytes 602120 | tf_op jit(solution)/shard_map/ppermute | solution.py:420
  231.3 8.5 %collective-permute-start.67 = (bf16[112,896]{1,0:T(8,128)(2,1)S(1)}, bf16[112,896]{1,0:T(8,128)(2,1)S(1)}, u32[]{:S(2)}, u32[]{:S(2)}) collective-permute-start(bf16[112,896]{1,0:T(8,128)(2,1)S(1)} %fusion.29), channel_id=1, source_target_pairs={{0,8},{2,6},{8,16},{10,2},{16,24},{18,10},{24,28},{26,18},{28,20},... | collective-permute-start | bytes 602120 | tf_op jit(solution)/shard_map/ppermute | solution.py:420
  233.5 8.5 %collective-permute-start.75 = (bf16[112,896]{1,0:T(8,128)(2,1)S(1)}, bf16[112,896]{1,0:T(8,128)(2,1)S(1)}, u32[]{:S(2)}, u32[]{:S(2)}) collective-permute-start(bf16[112,896]{1,0:T(8,128)(2,1)S(1)} %fusion.23), channel_id=1, source_target_pairs={{0,8},{2,6},{8,16},{10,2},{16,24},{18,10},{24,28},{26,18},{28,20},... | collective-permute-start | bytes 602120 | tf_op jit(solution)/shard_map/ppermute | solution.py:420
  237.8 8.5 %collective-permute-start.91 = (bf16[112,896]{1,0:T(8,128)(2,1)S(1)}, bf16[112,896]{1,0:T(8,128)(2,1)S(1)}, u32[]{:S(2)}, u32[]{:S(2)}) collective-permute-start(bf16[112,896]{1,0:T(8,128)(2,1)S(1)} %fusion.11), channel_id=1, source_target_pairs={{0,8},{2,6},{8,16},{10,2},{16,24},{18,10},{24,28},{26,18},{28,20},... | collective-permute-start | bytes 602120 | tf_op jit(solution)/shard_map/ppermute | solution.py:420
  240.0 8.5 %collective-permute-start.68 = (bf16[112,896]{1,0:T(8,128)(2,1)S(1)}, bf16[112,896]{1,0:T(8,128)(2,1)S(1)}, u32[]{:S(2)}, u32[]{:S(2)}) collective-permute-start(bf16[112,896]{1,0:T(8,128)(2,1)S(1)} %fusion.28), channel_id=1, source_target_pairs={{0,8},{2,6},{8,16},{10,2},{16,24},{18,10},{24,28},{26,18},{28,20},... | collective-permute-start | bytes 602120 | tf_op jit(solution)/shard_map/ppermute | solution.py:420
  242.1 8.5 %collective-permute-start.76 = (bf16[112,896]{1,0:T(8,128)(2,1)S(1)}, bf16[112,896]{1,0:T(8,128)(2,1)S(1)}, u32[]{:S(2)}, u32[]{:S(2)}) collective-permute-start(bf16[112,896]{1,0:T(8,128)(2,1)S(1)} %fusion.22), channel_id=1, source_target_pairs={{0,8},{2,6},{8,16},{10,2},{16,24},{18,10},{24,28},{26,18},{28,20},... | collective-permute-start | bytes 602120 | tf_op jit(solution)/shard_map/ppermute | solution.py:420
  244.2 8.5 %collective-permute-start.84 = (bf16[112,896]{1,0:T(8,128)(2,1)S(1)}, bf16[112,896]{1,0:T(8,128)(2,1)S(1)}, u32[]{:S(2)}, u32[]{:S(2)}) collective-permute-start(bf16[112,896]{1,0:T(8,128)(2,1)S(1)} %fusion.16), channel_id=1, source_target_pairs={{0,8},{2,6},{8,16},{10,2},{16,24},{18,10},{24,28},{26,18},{28,20},... | collective-permute-start | bytes 602120 | tf_op jit(solution)/shard_map/ppermute | solution.py:420
  246.4 8.5 %collective-permute-start.92 = (bf16[112,896]{1,0:T(8,128)(2,1)S(1)}, bf16[112,896]{1,0:T(8,128)(2,1)S(1)}, u32[]{:S(2)}, u32[]{:S(2)}) collective-permute-start(bf16[112,896]{1,0:T(8,128)(2,1)S(1)} %fusion.10), channel_id=1, source_target_pairs={{0,8},{2,6},{8,16},{10,2},{16,24},{18,10},{24,28},{26,18},{28,20},... | collective-permute-start | bytes 602120 | tf_op jit(solution)/shard_map/ppermute | solution.py:420
  248.6 8.5 %collective-permute-start.69 = (bf16[112,896]{1,0:T(8,128)(2,1)S(1)}, bf16[112,896]{1,0:T(8,128)(2,1)S(1)}, u32[]{:S(2)}, u32[]{:S(2)}) collective-permute-start(bf16[112,896]{1,0:T(8,128)(2,1)S(1)} %fusion.27), channel_id=1, source_target_pairs={{0,8},{2,6},{8,16},{10,2},{16,24},{18,10},{24,28},{26,18},{28,20},... | collective-permute-start | bytes 602120 | tf_op jit(solution)/shard_map/ppermute | solution.py:420
  250.7 8.5 %collective-permute-start.77 = (bf16[112,896]{1,0:T(8,128)(2,1)S(1)}, bf16[112,896]{1,0:T(8,128)(2,1)S(1)}, u32[]{:S(2)}, u32[]{:S(2)}) collective-permute-start(bf16[112,896]{1,0:T(8,128)(2,1)S(1)} %fusion.21), channel_id=1, source_target_pairs={{0,8},{2,6},{8,16},{10,2},{16,24},{18,10},{24,28},{26,18},{28,20},... | collective-permute-start | bytes 602120 | tf_op jit(solution)/shard_map/ppermute | solution.py:420
  252.8 8.5 %collective-permute-start.85 = (bf16[112,896]{1,0:T(8,128)(2,1)S(1)}, bf16[112,896]{1,0:T(8,128)(2,1)S(1)}, u32[]{:S(2)}, u32[]{:S(2)}) collective-permute-start(bf16[112,896]{1,0:T(8,128)(2,1)S(1)} %fusion.15), channel_id=1, source_target_pairs={{0,8},{2,6},{8,16},{10,2},{16,24},{18,10},{24,28},{26,18},{28,20},... | collective-permute-start | bytes 602120 | tf_op jit(solution)/shard_map/ppermute | solution.py:420
  255.0 8.5 %collective-permute-start.93 = (bf16[112,896]{1,0:T(8,128)(2,1)S(1)}, bf16[112,896]{1,0:T(8,128)(2,1)S(1)}, u32[]{:S(2)}, u32[]{:S(2)}) collective-permute-start(bf16[112,896]{1,0:T(8,128)(2,1)S(1)} %fusion.9), channel_id=1, source_target_pairs={{0,8},{2,6},{8,16},{10,2},{16,24},{18,10},{24,28},{26,18},{28,20},... | collective-permute-start | bytes 602120 | tf_op jit(solution)/shard_map/ppermute | solution.py:420
  259.3 8.5 %collective-permute-start.78 = (bf16[112,896]{1,0:T(8,128)(2,1)S(1)}, bf16[112,896]{1,0:T(8,128)(2,1)S(1)}, u32[]{:S(2)}, u32[]{:S(2)}) collective-permute-start(bf16[112,896]{1,0:T(8,128)(2,1)S(1)} %fusion.20), channel_id=1, source_target_pairs={{0,8},{2,6},{8,16},{10,2},{16,24},{18,10},{24,28},{26,18},{28,20},... | collective-permute-start | bytes 602120 | tf_op jit(solution)/shard_map/ppermute | solution.py:420
  265.8 8.5 %collective-permute-start.71 = (bf16[112,896]{1,0:T(8,128)(2,1)S(1)}, bf16[112,896]{1,0:T(8,128)(2,1)S(1)}, u32[]{:S(2)}, u32[]{:S(2)}) collective-permute-start(bf16[112,896]{1,0:T(8,128)(2,1)S(1)} %fusion.25), channel_id=1, source_target_pairs={{0,8},{2,6},{8,16},{10,2},{16,24},{18,10},{24,28},{26,18},{28,20},... | collective-permute-start | bytes 602120 | tf_op jit(solution)/shard_map/ppermute | solution.py:420
  267.9 8.5 %collective-permute-start.79 = (bf16[112,896]{1,0:T(8,128)(2,1)S(1)}, bf16[112,896]{1,0:T(8,128)(2,1)S(1)}, u32[]{:S(2)}, u32[]{:S(2)}) collective-permute-start(bf16[112,896]{1,0:T(8,128)(2,1)S(1)} %fusion.19), channel_id=1, source_target_pairs={{0,8},{2,6},{8,16},{10,2},{16,24},{18,10},{24,28},{26,18},{28,20},... | collective-permute-start | bytes 602120 | tf_op jit(solution)/shard_map/ppermute | solution.py:420
  272.2 8.5 %collective-permute-start.95 = (bf16[112,896]{1,0:T(8,128)(2,1)S(1)}, bf16[112,896]{1,0:T(8,128)(2,1)S(1)}, u32[]{:S(2)}, u32[]{:S(2)}) collective-permute-start(bf16[112,896]{1,0:T(8,128)(2,1)S(1)} %fusion.7), channel_id=1, source_target_pairs={{0,8},{2,6},{8,16},{10,2},{16,24},{18,10},{24,28},{26,18},{28,20},... | collective-permute-start | bytes 602120 | tf_op jit(solution)/shard_map/ppermute | solution.py:420
  (108 other events, 852.8 us)
